TPU v7x, 32 devices: a whole 2x2x4 slice. The times are simulated.
32 devices in a mesh: blk: 16 (over z, y, core), rep: 2 (over x).
Axes of the slice: x: 2, y: 2, z: 4, core: 2. Of those that a mesh axis runs over, the one named last changes fastest.
Arguments:
- features: bfloat16 [8192, 512], P(('blk', 'rep')), may hold values from -6 to 6
- tile_values: bfloat16 [16, 2, 96, 128, 128], P('blk', 'rep'), may hold values from -0.078125 to 0.078125
- tile_rows: int32 [16, 2, 96], P('blk', 'rep'), may hold values from 0 to 3, as said below
- tile_cols: int32 [16, 2, 96], P('blk', 'rep'), may hold values from 0 to 31, as said below
- tile_counts: int32 [16, 2], P('blk', 'rep'), may hold values from 21 to 96, as said below
- weight: bfloat16 [512, 512], replicated, may hold values from -0.25 to 0.25
- bias: float32 [512], replicated, may hold values from -3 to 3
- head: float32 [2, 512], replicated, may hold values from -0.125 to 0.125
- times: float32 [8192], P(('blk', 'rep')), may hold values from 0.3 to 3
- events: int32 [8192], P(('blk', 'rep')), may hold values 0 or 1
Outputs:
- hidden: bfloat16 [8192, 512], P(('blk', 'rep'))
- grad_weight: float32 [512, 512], replicated
- grad_bias: float32 [512], replicated
- grad_head: float32 [2, 512], replicated
Inputs may be any that keep to these rules, and one draw needn't show every extreme that they name: `tile_rows`: row tile of a slot within the row block of its device. `tile_cols`: within the live slots of one device no (row, column) pair repeats; each source block c is read by at most 6 live slots of one device, and by exactly 6 for some source block of every device. `tile_counts`: live slots come first, grouped by source block in increasing order of block; every source block has at least one live slot on every device; slots past the count hold arbitrary indices.
All inputs are finite; a program needn't handle non-finite values. No bound on the sum of `events` on one device may be relied on, other than what follows from the above.
Results may differ from a plain program's by a relative error of at most 0.0044.
Values may be sent and summed in bfloat16 or wider, within the bound.
A program may use at most 64 MiB of HBM per device.

v0:
```python
import math

import jax
import jax.numpy as jnp
from jax import lax
from jax.sharding import PartitionSpec as P

MOST = 6


def passed_along(value, axis, steps):
    count = lax.axis_size(axis)
    pairs = [(source, (source + steps) % count) for source in range(count)]
    return lax.ppermute(value, axis, pairs)


def run_bounds(col_ids, live_count, source, col_tiles):
    positions = jnp.arange(col_ids.shape[0])
    in_use = positions < live_count
    run_start = jnp.sum(in_use & (col_ids < source * col_tiles))
    run_stop = jnp.sum(in_use & (col_ids < (source + 1) * col_tiles))
    return (run_start, run_stop)


def add_capacity(partial_value, carried, source, tile_block, row_ids, col_ids, live_count):
    slots = tile_block.shape[0]
    tile_size = tile_block.shape[1]
    col_tiles = carried.shape[0] // tile_size
    run_start, run_stop = run_bounds(col_ids, live_count, source, col_tiles)
    window_start = jnp.minimum(run_start, slots - MOST)
    taken = lax.dynamic_slice_in_dim(tile_block, window_start, MOST, 0)
    picked_rows = lax.dynamic_slice_in_dim(row_ids, window_start, MOST, 0)
    picked_cols = lax.dynamic_slice_in_dim(col_ids, window_start, MOST, 0) % col_tiles
    slot_ids = window_start + jnp.arange(MOST)
    in_run = (slot_ids >= run_start) & (slot_ids < run_stop)
    selector = (picked_cols[:, None] == jnp.arange(col_tiles)[None, :]).astype(jnp.bfloat16)
    pieces = carried.reshape(col_tiles, tile_size, carried.shape[1])
    chosen = jnp.einsum("kc,ctf->ktf", selector, pieces, preferred_element_type=jnp.float32).astype(
        jnp.bfloat16
    )
    products = jnp.einsum("kij,kjf->kif", taken, chosen, preferred_element_type=jnp.float32)
    products = products * in_run[:, None, None].astype(jnp.float32)
    return partial_value.at[picked_rows].add(products)


def local(
    features, tile_values, tile_rows, tile_cols, tile_counts, weight, bias, head, times, events
):
    tile_block = tile_values[0, 0]
    row_ids = tile_rows[0, 0]
    col_ids = tile_cols[0, 0]
    live_count = tile_counts[0, 0]
    rows_here, feature_width = features.shape
    tile_size = tile_block.shape[1]
    replicas = lax.axis_size("rep")
    owners = lax.axis_size("blk")
    row_tiles = rows_here * replicas // tile_size
    partial_value = jnp.zeros((row_tiles, tile_size, feature_width), jnp.float32)

    def accumulate(accum, carried, source):
        return add_capacity(accum, carried, source, tile_block, row_ids, col_ids, live_count)

    owner = lax.axis_index("blk")
    partial_value = accumulate(partial_value, features, owner)

    def advance(cycle_step, state):
        accum, carried = state
        carried = passed_along(carried, "blk", 1)
        source = (owner - cycle_step) % owners
        return (accumulate(accum, carried, source), carried)

    partial_value, unused = lax.fori_loop(1, owners, advance, (partial_value, features))
    summed = lax.psum_scatter(
        partial_value.reshape(row_tiles * tile_size, feature_width),
        "rep",
        scatter_dimension=0,
        tiled=True,
    )
    aggregated_bf = summed.astype(jnp.bfloat16)
    preact = jnp.dot(aggregated_bf, weight, preferred_element_type=jnp.float32) + bias
    hidden = jax.nn.silu(preact).astype(jnp.bfloat16)
    hidden_wide = lax.optimization_barrier(hidden).astype(jnp.float32)
    scores = jnp.dot(hidden_wide, head.T, precision=lax.Precision.HIGHEST)
    scale_log = scores[:, 0]
    shape_param = jax.nn.softplus(scores[:, 1]) + 0.5
    log_ratio = jnp.log(times) - scale_log
    hazard = jnp.exp(shape_param * log_ratio)
    observed = events.astype(jnp.float32)
    norm_factor = 1.0 / math.sqrt(rows_here * owners * replicas)
    grad_scale = (observed * shape_param - shape_param * hazard) * norm_factor
    grad_shape = (
        (hazard * log_ratio - observed * (1.0 / shape_param + log_ratio))
        * jax.nn.sigmoid(scores[:, 1])
        * norm_factor
    )
    stacked = jnp.stack([grad_scale, grad_shape], axis=1)
    grad_head = jnp.dot(stacked.T, hidden_wide, precision=lax.Precision.HIGHEST)
    sigmoid_pre = jax.nn.sigmoid(preact)
    grad_hidden = grad_scale[:, None] * head[0][None, :] + grad_shape[:, None] * head[1][None, :]
    grad_preact = grad_hidden * sigmoid_pre * (1.0 + preact * (1.0 - sigmoid_pre))
    grad_bias = jnp.sum(grad_preact, axis=0)
    grad_preact_bf = grad_preact.astype(jnp.bfloat16)
    grad_weight = lax.dot_general(
        aggregated_bf, grad_preact_bf, (((0,), (0,)), ((), ())), preferred_element_type=jnp.float32
    )
    totals = lax.psum((grad_weight, grad_bias, grad_head), ("blk", "rep"))
    return (hidden, totals[0], totals[1], totals[2])


def solution(mesh):
    placed = (
        P(("blk", "rep"), None),
        P("blk", "rep", None, None, None),
        P("blk", "rep", None),
        P("blk", "rep", None),
        P("blk", "rep"),
        P(),
        P(),
        P(),
        P(("blk", "rep")),
        P(("blk", "rep")),
    )
    return jax.shard_map(
        local,
        mesh=mesh,
        in_specs=placed,
        out_specs=(P(("blk", "rep"), None), P(), P(), P()),
        check_vma=False,
    )
```

profile of v0, /device:TPU:1, one launch (start us, length us, event | category | flops | bytes accessed | tf_op | source)
XLA Modules:
  0.0 365.4 jit_solution(12173868850932725826)
XLA Ops:
  17.6 177.1 %while.18 = (s32[]{:T(128)}, f32[4,128,512]{2,1,0:T(8,128)S(1)}, bf16[256,512]{1,0:T(8,128)(2,1)S(1)}, s32[]{:T(128)}, s32[]{:T(128)}, /*index=5*/s32[96]{0:T(12...) while((s32[]{:T(128)}, f32[4,128,512]{2,1,0:T(8,128)S(1)}, ...), condition=%wide.region_7.8_spmd, body=%wide.region_3.7_spmd.sunk | while | flops 103023600 | bytes 9896936 | solution.py:72
  17.6 2.7 collective-permute-start
  24.1 1.6 convolution_multiply_fusion.3
  27.3 2.5 collective-permute-start
  36.8 2.5 collective-permute-start
  44.7 1.6 convolution_multiply_fusion.3
  52.2 4.2 %collective-permute-done = bf16[256,512]{1,0:T(8,128)(2,1)S(1)} collective-permute-done((bf16[256,512]{1,0:T(8,128)(2,1)S(1)}, bf16[256,512]{1,0:T(8,128)(2,1)S(1)}, u32[]{:S(2)}, u32[]{:S(2)}) %collective-permute-start) | collective-permute-done | bytes 262176 | tf_op jit(solution)/shard_map/while/body/eval_jaxpr/ppermute | solution.py:14
  63.6 5.1 %collective-permute-done = bf16[256,512]{1,0:T(8,128)(2,1)S(1)} collective-permute-done((bf16[256,512]{1,0:T(8,128)(2,1)S(1)}, bf16[256,512]{1,0:T(8,128)(2,1)S(1)}, u32[]{:S(2)}, u32[]{:S(2)}) %collective-permute-start) | collective-permute-done | bytes 262176 | tf_op jit(solution)/shard_map/while/body/eval_jaxpr/ppermute | solution.py:14
  69.2 1.6 convolution_multiply_fusion.3
  75.8 5.1 %collective-permute-done = bf16[256,512]{1,0:T(8,128)(2,1)S(1)} collective-permute-done((bf16[256,512]{1,0:T(8,128)(2,1)S(1)}, bf16[256,512]{1,0:T(8,128)(2,1)S(1)}, u32[]{:S(2)}, u32[]{:S(2)}) %collective-permute-start) | collective-permute-done | bytes 262176 | tf_op jit(solution)/shard_map/while/body/eval_jaxpr/ppermute | solution.py:14
  88.0 5.1 %collective-permute-done = bf16[256,512]{1,0:T(8,128)(2,1)S(1)} collective-permute-done((bf16[256,512]{1,0:T(8,128)(2,1)S(1)}, bf16[256,512]{1,0:T(8,128)(2,1)S(1)}, u32[]{:S(2)}, u32[]{:S(2)}) %collective-permute-start) | collective-permute-done | bytes 262176 | tf_op jit(solution)/shard_map/while/body/eval_jaxpr/ppermute | solution.py:14
  93.6 1.6 convolution_multiply_fusion.3
  100.3 5.1 %collective-permute-done = bf16[256,512]{1,0:T(8,128)(2,1)S(1)} collective-permute-done((bf16[256,512]{1,0:T(8,128)(2,1)S(1)}, bf16[256,512]{1,0:T(8,128)(2,1)S(1)}, u32[]{:S(2)}, u32[]{:S(2)}) %collective-permute-start) | collective-permute-done | bytes 262176 | tf_op jit(solution)/shard_map/while/body/eval_jaxpr/ppermute | solution.py:14
  112.5 5.1 %collective-permute-done = bf16[256,512]{1,0:T(8,128)(2,1)S(1)} collective-permute-done((bf16[256,512]{1,0:T(8,128)(2,1)S(1)}, bf16[256,512]{1,0:T(8,128)(2,1)S(1)}, u32[]{:S(2)}, u32[]{:S(2)}) %collective-permute-start) | collective-permute-done | bytes 262176 | tf_op jit(solution)/shard_map/while/body/eval_jaxpr/ppermute | solution.py:14
  124.7 5.1 %collective-permute-done = bf16[256,512]{1,0:T(8,128)(2,1)S(1)} collective-permute-done((bf16[256,512]{1,0:T(8,128)(2,1)S(1)}, bf16[256,512]{1,0:T(8,128)(2,1)S(1)}, u32[]{:S(2)}, u32[]{:S(2)}) %collective-permute-start) | collective-permute-done | bytes 262176 | tf_op jit(solution)/shard_map/while/body/eval_jaxpr/ppermute | solution.py:14
  136.9 5.1 %collective-permute-done = bf16[256,512]{1,0:T(8,128)(2,1)S(1)} collective-permute-done((bf16[256,512]{1,0:T(8,128)(2,1)S(1)}, bf16[256,512]{1,0:T(8,128)(2,1)S(1)}, u32[]{:S(2)}, u32[]{:S(2)}) %collective-permute-start) | collective-permute-done | bytes 262176 | tf_op jit(solution)/shard_map/while/body/eval_jaxpr/ppermute | solution.py:14
  149.2 5.1 %collective-permute-done = bf16[256,512]{1,0:T(8,128)(2,1)S(1)} collective-permute-done((bf16[256,512]{1,0:T(8,128)(2,1)S(1)}, bf16[256,512]{1,0:T(8,128)(2,1)S(1)}, u32[]{:S(2)}, u32[]{:S(2)}) %collective-permute-start) | collective-permute-done | bytes 262176 | tf_op jit(solution)/shard_map/while/body/eval_jaxpr/ppermute | solution.py:14
  161.4 5.1 %collective-permute-done = bf16[256,512]{1,0:T(8,128)(2,1)S(1)} collective-permute-done((bf16[256,512]{1,0:T(8,128)(2,1)S(1)}, bf16[256,512]{1,0:T(8,128)(2,1)S(1)}, u32[]{:S(2)}, u32[]{:S(2)}) %collective-permute-start) | collective-permute-done | bytes 262176 | tf_op jit(solution)/shard_map/while/body/eval_jaxpr/ppermute | solution.py:14
  173.6 5.1 %collective-permute-done = bf16[256,512]{1,0:T(8,128)(2,1)S(1)} collective-permute-done((bf16[256,512]{1,0:T(8,128)(2,1)S(1)}, bf16[256,512]{1,0:T(8,128)(2,1)S(1)}, u32[]{:S(2)}, u32[]{:S(2)}) %collective-permute-start) | collective-permute-done | bytes 262176 | tf_op jit(solution)/shard_map/while/body/eval_jaxpr/ppermute | solution.py:14
  185.9 5.1 %collective-permute-done = bf16[256,512]{1,0:T(8,128)(2,1)S(1)} collective-permute-done((bf16[256,512]{1,0:T(8,128)(2,1)S(1)}, bf16[256,512]{1,0:T(8,128)(2,1)S(1)}, u32[]{:S(2)}, u32[]{:S(2)}) %collective-permute-start) | collective-permute-done | bytes 262176 | tf_op jit(solution)/shard_map/while/body/eval_jaxpr/ppermute | solution.py:14
  195.8 24.8 %reduce-scatter.2.cloned.1.call-done = f32[256,512]{1,0:T(8,128)} async-done(((f32[512,512]{1,0:T(8,128)}), f32[256,512]{1,0:T(8,128)}) %reduce-scatter.2.cloned.1.call-update) | async-done | bytes 524304 | tf_op jit(solution)/shard_map/reduce_scatter | solution.py:73
  224.5 39.3 %all-reduce = (f32[512]{0:T(512)}, f32[2,512]{1,0:T(2,128)}) all-reduce(f32[512]{0:T(512)S(1)} %fusion.36, f32[2,512]{1,0:T(2,128)S(1)} %fusion.20), channel_id=1, replica_groups=mesh['blk'=16,'rep'=2] {'blk','rep'}, use_global_device_ids=true, to_apply=%region_11.12 | all-reduce | flops 1536 | bytes 12288 | tf_op jit(solution)/shard_map/psum | solution.py:106
  263.8 92.5 %all-reduce.3.cloned.1.call-done = f32[512,512]{1,0:T(8,128)} async-done(((f32[512,512]{1,0:T(8,128)}), f32[512,512]{1,0:T(8,128)}) %all-reduce.3.cloned.1.call-update) | async-done | bytes 1048592 | tf_op jit(solution)/shard_map/psum | solution.py:106
  356.3 2.3 copy.45
  (157 shorter events, 105.2 us)
Async XLA Ops:
  7.2 213.4 %copy-start = (bf16[512,512]{1,0:T(8,128)(2,1)S(1)}, bf16[512,512]{1,0:T(8,128)(2,1)}, u32[]{:S(2)}) copy-start(bf16[512,512]{1,0:T(8,128)(2,1)} %param.17) | copy-start | bytes 1572868
  7.2 213.4 %reduce-scatter.2.cloned.1.call-start = ((), (), s32[]{:S(2)}) async-start(), calls=%async_computation.1 | async-start | bytes 1572864 | tf_op jit(solution)/shard_map/reduce_scatter | solution.py:73
  17.6 178.1 %copy-start.4 = (f32[2,512]{1,0:T(2,128)S(1)}, f32[2,512]{1,0:T(2,128)}, u32[]{:S(2)}) copy-start(f32[2,512]{1,0:T(2,128)} %param.19) | copy-start | bytes 12292
  17.6 203.0 %copy-start.9 = (f32[512]{0:T(512)S(1)}, f32[512]{0:T(512)}, u32[]{:S(2)}) copy-start(f32[512]{0:T(512)} %param.18) | copy-start | bytes 6148
  17.6 6.0 %collective-permute-start = (bf16[256,512]{1,0:T(8,128)(2,1)S(1)}, bf16[256,512]{1,0:T(8,128)(2,1)S(1)}, u32[]{:S(2)}, u32[]{:S(2)}) collective-permute-start(bf16[256,512]{1,0:T(8,128)(2,1)S(1)} %get-tuple-element.337), channel_id=1, source_target_pairs={{0,2},{2,4},{4,6},{6,8},{8,10},{10,12},{12,14},{14,16},{16,18},{18... | collective-permute-start | bytes 786440 | tf_op jit(solution)/shard_map/while/body/eval_jaxpr/ppermute | solution.py:14
  27.3 5.9 %collective-permute-start = (bf16[256,512]{1,0:T(8,128)(2,1)S(1)}, bf16[256,512]{1,0:T(8,128)(2,1)S(1)}, u32[]{:S(2)}, u32[]{:S(2)}) collective-permute-start(bf16[256,512]{1,0:T(8,128)(2,1)S(1)} %get-tuple-element.337), channel_id=1, source_target_pairs={{0,2},{2,4},{4,6},{6,8},{8,10},{10,12},{12,14},{14,16},{16,18},{18... | collective-permute-start | bytes 786440 | tf_op jit(solution)/shard_map/while/body/eval_jaxpr/ppermute | solution.py:14
  36.8 7.4 %collective-permute-start = (bf16[256,512]{1,0:T(8,128)(2,1)S(1)}, bf16[256,512]{1,0:T(8,128)(2,1)S(1)}, u32[]{:S(2)}, u32[]{:S(2)}) collective-permute-start(bf16[256,512]{1,0:T(8,128)(2,1)S(1)} %get-tuple-element.337), channel_id=1, source_target_pairs={{0,2},{2,4},{4,6},{6,8},{8,10},{10,12},{12,14},{14,16},{16,18},{18... | collective-permute-start | bytes 786440 | tf_op jit(solution)/shard_map/while/body/eval_jaxpr/ppermute | solution.py:14
  47.9 8.6 %collective-permute-start = (bf16[256,512]{1,0:T(8,128)(2,1)S(1)}, bf16[256,512]{1,0:T(8,128)(2,1)S(1)}, u32[]{:S(2)}, u32[]{:S(2)}) collective-permute-start(bf16[256,512]{1,0:T(8,128)(2,1)S(1)} %get-tuple-element.337), channel_id=1, source_target_pairs={{0,2},{2,4},{4,6},{6,8},{8,10},{10,12},{12,14},{14,16},{16,18},{18... | collective-permute-start | bytes 786440 | tf_op jit(solution)/shard_map/while/body/eval_jaxpr/ppermute | solution.py:14
  60.1 8.5 %collective-permute-start = (bf16[256,512]{1,0:T(8,128)(2,1)S(1)}, bf16[256,512]{1,0:T(8,128)(2,1)S(1)}, u32[]{:S(2)}, u32[]{:S(2)}) collective-permute-start(bf16[256,512]{1,0:T(8,128)(2,1)S(1)} %get-tuple-element.337), channel_id=1, source_target_pairs={{0,2},{2,4},{4,6},{6,8},{8,10},{10,12},{12,14},{14,16},{16,18},{18... | collective-permute-start | bytes 786440 | tf_op jit(solution)/shard_map/while/body/eval_jaxpr/ppermute | solution.py:14
  72.4 8.5 %collective-permute-start = (bf16[256,512]{1,0:T(8,128)(2,1)S(1)}, bf16[256,512]{1,0:T(8,128)(2,1)S(1)}, u32[]{:S(2)}, u32[]{:S(2)}) collective-permute-start(bf16[256,512]{1,0:T(8,128)(2,1)S(1)} %get-tuple-element.337), channel_id=1, source_target_pairs={{0,2},{2,4},{4,6},{6,8},{8,10},{10,12},{12,14},{14,16},{16,18},{18... | collective-permute-start | bytes 786440 | tf_op jit(solution)/shard_map/while/body/eval_jaxpr/ppermute | solution.py:14
  84.6 8.5 %collective-permute-start = (bf16[256,512]{1,0:T(8,128)(2,1)S(1)}, bf16[256,512]{1,0:T(8,128)(2,1)S(1)}, u32[]{:S(2)}, u32[]{:S(2)}) collective-permute-start(bf16[256,512]{1,0:T(8,128)(2,1)S(1)} %get-tuple-element.337), channel_id=1, source_target_pairs={{0,2},{2,4},{4,6},{6,8},{8,10},{10,12},{12,14},{14,16},{16,18},{18... | collective-permute-start | bytes 786440 | tf_op jit(solution)/shard_map/while/body/eval_jaxpr/ppermute | solution.py:14
  96.8 8.5 %collective-permute-start = (bf16[256,512]{1,0:T(8,128)(2,1)S(1)}, bf16[256,512]{1,0:T(8,128)(2,1)S(1)}, u32[]{:S(2)}, u32[]{:S(2)}) collective-permute-start(bf16[256,512]{1,0:T(8,128)(2,1)S(1)} %get-tuple-element.337), channel_id=1, source_target_pairs={{0,2},{2,4},{4,6},{6,8},{8,10},{10,12},{12,14},{14,16},{16,18},{18... | collective-permute-start | bytes 786440 | tf_op jit(solution)/shard_map/while/body/eval_jaxpr/ppermute | solution.py:14
  109.1 8.5 %collective-permute-start = (bf16[256,512]{1,0:T(8,128)(2,1)S(1)}, bf16[256,512]{1,0:T(8,128)(2,1)S(1)}, u32[]{:S(2)}, u32[]{:S(2)}) collective-permute-start(bf16[256,512]{1,0:T(8,128)(2,1)S(1)} %get-tuple-element.337), channel_id=1, source_target_pairs={{0,2},{2,4},{4,6},{6,8},{8,10},{10,12},{12,14},{14,16},{16,18},{18... | collective-permute-start | bytes 786440 | tf_op jit(solution)/shard_map/while/body/eval_jaxpr/ppermute | solution.py:14
  121.3 8.6 %collective-permute-start = (bf16[256,512]{1,0:T(8,128)(2,1)S(1)}, bf16[256,512]{1,0:T(8,128)(2,1)S(1)}, u32[]{:S(2)}, u32[]{:S(2)}) collective-permute-start(bf16[256,512]{1,0:T(8,128)(2,1)S(1)} %get-tuple-element.337), channel_id=1, source_target_pairs={{0,2},{2,4},{4,6},{6,8},{8,10},{10,12},{12,14},{14,16},{16,18},{18... | collective-permute-start | bytes 786440 | tf_op jit(solution)/shard_map/while/body/eval_jaxpr/ppermute | solution.py:14
  133.5 8.5 %collective-permute-start = (bf16[256,512]{1,0:T(8,128)(2,1)S(1)}, bf16[256,512]{1,0:T(8,128)(2,1)S(1)}, u32[]{:S(2)}, u32[]{:S(2)}) collective-permute-start(bf16[256,512]{1,0:T(8,128)(2,1)S(1)} %get-tuple-element.337), channel_id=1, source_target_pairs={{0,2},{2,4},{4,6},{6,8},{8,10},{10,12},{12,14},{14,16},{16,18},{18... | collective-permute-start | bytes 786440 | tf_op jit(solution)/shard_map/while/body/eval_jaxpr/ppermute | solution.py:14
  145.8 8.5 %collective-permute-start = (bf16[256,512]{1,0:T(8,128)(2,1)S(1)}, bf16[256,512]{1,0:T(8,128)(2,1)S(1)}, u32[]{:S(2)}, u32[]{:S(2)}) collective-permute-start(bf16[256,512]{1,0:T(8,128)(2,1)S(1)} %get-tuple-element.337), channel_id=1, source_target_pairs={{0,2},{2,4},{4,6},{6,8},{8,10},{10,12},{12,14},{14,16},{16,18},{18... | collective-permute-start | bytes 786440 | tf_op jit(solution)/shard_map/while/body/eval_jaxpr/ppermute | solution.py:14
  158.0 8.6 %collective-permute-start = (bf16[256,512]{1,0:T(8,128)(2,1)S(1)}, bf16[256,512]{1,0:T(8,128)(2,1)S(1)}, u32[]{:S(2)}, u32[]{:S(2)}) collective-permute-start(bf16[256,512]{1,0:T(8,128)(2,1)S(1)} %get-tuple-element.337), channel_id=1, source_target_pairs={{0,2},{2,4},{4,6},{6,8},{8,10},{10,12},{12,14},{14,16},{16,18},{18... | collective-permute-start | bytes 786440 | tf_op jit(solution)/shard_map/while/body/eval_jaxpr/ppermute | solution.py:14
  170.2 8.5 %collective-permute-start = (bf16[256,512]{1,0:T(8,128)(2,1)S(1)}, bf16[256,512]{1,0:T(8,128)(2,1)S(1)}, u32[]{:S(2)}, u32[]{:S(2)}) collective-permute-start(bf16[256,512]{1,0:T(8,128)(2,1)S(1)} %get-tuple-element.337), channel_id=1, source_target_pairs={{0,2},{2,4},{4,6},{6,8},{8,10},{10,12},{12,14},{14,16},{16,18},{18... | collective-permute-start | bytes 786440 | tf_op jit(solution)/shard_map/while/body/eval_jaxpr/ppermute | solution.py:14
  182.4 8.6 %collective-permute-start = (bf16[256,512]{1,0:T(8,128)(2,1)S(1)}, bf16[256,512]{1,0:T(8,128)(2,1)S(1)}, u32[]{:S(2)}, u32[]{:S(2)}) collective-permute-start(bf16[256,512]{1,0:T(8,128)(2,1)S(1)} %get-tuple-element.337), channel_id=1, source_target_pairs={{0,2},{2,4},{4,6},{6,8},{8,10},{10,12},{12,14},{14,16},{16,18},{18... | collective-permute-start | bytes 786440 | tf_op jit(solution)/shard_map/while/body/eval_jaxpr/ppermute | solution.py:14
  195.7 160.6 %all-reduce.3.cloned.1.call-start = ((), (), s32[]{:S(2)}) async-start(), calls=%async_computation.2 | async-start | bytes 2097152 | tf_op jit(solution)/shard_map/psum | solution.py:106
  195.7 26.6 %copy-start.6 = (s32[256]{0:T(256)S(1)}, s32[256]{0:T(256)}, u32[]{:S(2)}) copy-start(s32[256]{0:T(256)} %param.21) | copy-start | bytes 3076
  195.7 26.6 %copy-start.7 = (f32[256]{0:T(256)S(1)}, f32[256]{0:T(256)}, u32[]{:S(2)}) copy-start(f32[256]{0:T(256)} %param.20) | copy-start | bytes 3076
  220.5 1.9 copy-start.8
  222.0 2.2 copy-start.2
  (3 other events, 4.1 us)
Sparse Core Ops, SparseCore 0:
  195.8 24.7 reduce-scatter.1
  227.1 129.1 all-reduce.2
where the time goes:
time: 368 us; the launch traced here: 365 us
  waiting for transfers between devices  180 us (49%)
  other arithmetic  69.1 us (19%)
  blocking collectives  39.3 us (11%)
  matrix products  36.8 us (10%)
  between operations  15.6 us (4%)
  loops' own time  10.9 us (3%)
  starting transfers between devices  9.43 us (3%)
  local copies, waits for them, and re-layouts  4.72 us (1%)
    psum x1, waiting for transfers between devices, local(): totals = lax.psum((grad_weight, grad_bias, grad_head), ('blk', 'rep'))  92.5 us
    ppermute x15, waiting for transfers between devices, passed_along(): return lax.ppermute(value, axis, pairs)  62.2 us
    psum x1, blocking collectives, local(): totals = lax.psum((grad_weight, grad_bias, grad_head), ('blk', 'rep'))  39.3 us
    dot_general x16, matrix products, add_capacity(): jnp.einsum('kij,kjf->kif', taken, chosen, preferred_element_type=jnp.floa...  25.5 us
    reduce_scatter x1, waiting for transfers between devices, local(): lax.psum_scatter(partial_value.reshape(row_tiles * tile_size, feature_wid...  24.8 us
    scatter-add x16, other arithmetic, add_capacity(): return partial_value.at[picked_rows].add(products)  24.7 us
    convert_element_type x16, other arithmetic, add_capacity(): products = products * in_run[:, None, None].astype(jnp.float32)  20.8 us
    reduce_sum x16, other arithmetic, run_bounds(): run_stop = jnp.sum(in_use & (col_ids < (source + 1) * col_tiles))  20.6 us
  transfers between devices with their start and end apart: 17, of which 15 were waited for; matrix products, arithmetic and copies ran while one was open for 11% of the time, Pallas kernels for 0%

commit v1 on v0

v1 whole, which is shorter than its diff:
```python
import functools
import math

import jax
import jax.numpy as jnp
from jax import lax
from jax.experimental import pallas as pl
from jax.experimental.pallas import tpu as pltpu
from jax.sharding import PartitionSpec as P

MOST = 6
MESH = pl.DeviceIdType.MESH
F32 = jnp.float32
BF16 = jnp.bfloat16


def fused_sum_rows(owners, replicas, width):
    group = 2 * replicas
    line = owners // 4
    half = width // 2
    if owners % 4 or half % (group * line) or (half // (group * line)) % 16:
        return None
    return half, half // group, half // (group * line)


def kernel(
    owners, replicas, pieces,
    feats, tiles_hbm, rows_ref, cols_ref, count_ref, weight_hbm, bias_ref, head_ref, times_ref, events_ref,
    hidden_ref, gw_ref, small_ref,
    gath, dense, tiles, weight, acc, xsend, xrecv, agg, pre, slope,
    gsum, g1s, g1r, g2s, g2r, g3s, g3r, sm_send, sm1, sm2, sm3,
    local_sem, ring_send, ring_recv, mate_send, mate_recv, x_send, x_recv, g_send, g_recv, s_send, s_recv,
):
    chips = owners // 2
    far = chips // 2
    slots = tiles_hbm.shape[0]
    tile = tiles_hbm.shape[1]
    here = feats.shape[0]
    width = feats.shape[1]
    half = width // 2
    col_tiles = here // tile
    row_tiles = here * replicas // tile
    unit = here // 2

    b = lax.axis_index("blk")
    r = lax.axis_index("rep")
    core = lax.rem(b, 2)
    chip = lax.div(b, 2)
    y = lax.rem(chip, 2)
    z = lax.div(chip, 2)
    pos = (1 - y) * z + y * (chips - 1 - z)
    mate = chip * 2 + 1 - core

    def block_at(position):
        upper = lax.div(position, far)
        depth = (1 - upper) * position + upper * (chips - 1 - position)
        return (2 * depth + upper) * 2 + core

    def from_me(d, h):
        return block_at(lax.rem(pos + (chips - h if d == 0 else h), chips))

    def mate_of(block):
        return block + 1 - 2 * core

    right, left = from_me(1, 1), from_me(0, 1)

    def reach(d, u):
        return far if d == u else far - 1

    def ring(d, s, u, h, block):
        ref = gath.at[s, block, pl.ds(u * unit, unit)]
        return pltpu.make_async_remote_copy(
            src_ref=ref, dst_ref=ref,
            send_sem=ring_send.at[d, s, u, h], recv_sem=ring_recv.at[d, s, u, h],
            device_id=(right if d == 0 else left, r), device_id_type=MESH,
        )

    def to_mate(d, s, u, h, block):
        ref = gath.at[s, block, pl.ds(u * unit, unit)]
        return pltpu.make_async_remote_copy(
            src_ref=ref, dst_ref=ref,
            send_sem=mate_send.at[d, s, u, h], recv_sem=mate_recv.at[d, s, u, h],
            device_id=(mate, r), device_id_type=MESH,
        )

    own = [pltpu.make_async_copy(feats.at[:, pl.ds(s * half, half)], gath.at[s, b], local_sem.at[s]) for s in range(2)]
    own[0].start()
    own[1].start()
    get_tiles = pltpu.make_async_copy(tiles_hbm, tiles.at[pl.ds(0, slots)], local_sem.at[2])
    get_tiles.start()
    get_weight = pltpu.make_async_copy(weight_hbm, weight, local_sem.at[3])
    get_weight.start()

    group = 2 * replicas
    line = owners // 4
    in_group = y * replicas + r

    def group_peer(o):
        other = lax.rem(in_group + o, group)
        return ((z * 2 + lax.div(other, replicas)) * 2 + core, lax.rem(other, replicas))

    def line_peer(o):
        return ((lax.rem(z + o, line) * 2 + y) * 2 + core, r)

    greeted = [(right, r), (left, r), (mate, r)]
    greeted += [(b, lax.rem(r + o, replicas)) for o in range(1, replicas)]
    if pieces:
        greeted += [group_peer(o) for o in range(1, group)] + [line_peer(o) for o in range(1, line)]
    barrier = pltpu.get_barrier_semaphore()
    for peer in greeted:
        pl.semaphore_signal(barrier, inc=1, device_id=peer, device_id_type=MESH)
    pl.semaphore_wait(barrier, len(greeted))

    sent = []

    def start(copy):
        copy.start()
        sent.append(copy)

    def send_own(s):
        for u in range(2):
            for d in range(2):
                start(ring(d, s, u, 0, b))
        for u in range(2):
            start(to_mate(0, s, u, 0, b))

    def arrive(s, h):
        for u in range(2):
            for d in range(2):
                if h > reach(d, u):
                    continue
                block = from_me(d, h)
                ring(d, s, u, h - 1, block).wait_recv()
                if h + 1 <= reach(d, u):
                    start(ring(d, s, u, h, block))
                start(to_mate(d, s, u, h, block))

    def arrive_mate(s, h):
        for u in range(2):
            for d in range(2):
                if h == 0:
                    if d == 0:
                        to_mate(0, s, u, 0, mate).wait_recv()
                elif h <= reach(d, u):
                    to_mate(d, s, u, h, mate_of(from_me(d, h))).wait_recv()

    tiles[slots] = jnp.zeros((tile, tile), BF16)
    count = count_ref[0, 0]

    def fill(source, first):
        picked = [jnp.int32(slots)] * (row_tiles * col_tiles)
        run = jnp.int32(0)
        for k in range(MOST):
            slot = first + k
            safe = jnp.minimum(slot, slots - 1)
            q = cols_ref[0, 0, safe]
            ok = (slot < count) & (q >= source * col_tiles) & (q < (source + 1) * col_tiles)
            key = jnp.where(ok, rows_ref[0, 0, safe] * col_tiles + q - source * col_tiles, -1)
            run = run + ok.astype(jnp.int32)
            picked = [jnp.where(key == at, slot, old) for at, old in enumerate(picked)]
        for at, slot in enumerate(picked):
            i, j = at // col_tiles, at % col_tiles
            dense[source, i * tile:(i + 1) * tile, j * tile:(j + 1) * tile] = tiles[slot]
        return first + run

    def product(s, part, block):
        a = dense[block, pl.ds(pl.multiple_of(part * here, here), here), :]
        return jnp.dot(a, gath[s, block], preferred_element_type=F32)

    def multiply(s, part, blocks):
        total = acc[s, part]
        for block in blocks:
            total = total + product(s, part, block)
        acc[s, part] = total

    def blocks_at(h):
        if h == 0:
            return [b, mate]
        ones = [from_me(0, h)] if h == far else [from_me(0, h), from_me(1, h)]
        return ones + [mate_of(block) for block in ones]

    def to_rep(s, o):
        return pltpu.make_async_remote_copy(
            src_ref=xsend.at[s, o - 1], dst_ref=xrecv.at[s, o - 1],
            send_sem=x_send.at[s, o - 1], recv_sem=x_recv.at[s, o - 1],
            device_id=(b, lax.rem(r + o, replicas)), device_id_type=MESH,
        )

    def settle(s):
        total = acc[s, r]
        for o in range(1, replicas):
            to_rep(s, o).wait_recv()
            total = total + xrecv[s, o - 1].astype(F32)
        agg[s] = total.astype(BF16)

    own[0].wait()
    own[1].wait()
    send_own(0)
    get_tiles.wait()
    first = jnp.int32(0)
    share = owners // far
    for h in range(1, far + 1):
        first = lax.fori_loop((h - 1) * share, h * share, fill, first)
        arrive(0, h)
        if h == far - 1:
            send_own(1)
    for h in range(far + 1):
        arrive_mate(0, h)
    arrive(1, 1)

    def first_half(part):
        def step(block, total):
            return total + product(0, part, block)
        return lax.fori_loop(0, owners, step, jnp.zeros((here, half), F32))

    for o in range(1, replicas):
        xsend[0, o - 1] = first_half(lax.rem(r + o, replicas)).astype(BF16)
        start(to_rep(0, o))
    acc[0, r] = first_half(r)

    arrive(1, 2)
    acc[1] = jnp.zeros((replicas, here, half), F32)
    for h in range(2):
        arrive_mate(1, h)
        for part in range(replicas):
            multiply(1, part, blocks_at(h))
    settle(0)
    get_weight.wait()
    pre[...] = jnp.dot(agg[0], weight[0:half, :], preferred_element_type=F32) + bias_ref[...]
    for h in range(3, far + 1):
        arrive(1, h)
        arrive_mate(1, h - 1)
        for part in range(replicas):
            multiply(1, part, blocks_at(h - 1))
    arrive_mate(1, far)
    for o in range(1, replicas):
        part = lax.rem(r + o, replicas)
        multiply(1, part, blocks_at(far))
        xsend[1, o - 1] = acc[1, part].astype(BF16)
        start(to_rep(1, o))
    multiply(1, r, blocks_at(far))
    settle(1)

    rows = 64
    for at in range(0, here, rows):
        p = pre[at:at + rows, :] + jnp.dot(agg[1, at:at + rows, :], weight[half:, :], preferred_element_type=F32)
        sig = 1.0 / (1.0 + jnp.exp(-p))
        hidden_ref[at:at + rows, :] = (p * sig).astype(BF16)
        slope[at:at + rows, :] = sig * (1.0 + p * (1.0 - sig))
    wide = hidden_ref[...].astype(F32)
    scores = lax.dot_general(
        head_ref[...], wide, (((1,), (1,)), ((), ())), precision=lax.Precision.HIGHEST, preferred_element_type=F32
    )
    scale_log = scores[0:1, :]
    raw = scores[1:2, :]
    shape_param = jnp.maximum(raw, 0.0) + jnp.log1p(jnp.exp(-jnp.abs(raw))) + 0.5
    log_ratio = jnp.log(times_ref[...]) - scale_log
    hazard = jnp.exp(shape_param * log_ratio)
    observed = events_ref[...].astype(F32)
    norm = 1.0 / math.sqrt(here * owners * replicas)
    grad_scale = (observed * shape_param - shape_param * hazard) * norm
    grad_shape = (
        (hazard * log_ratio - observed * (1.0 / shape_param + log_ratio)) * (1.0 / (1.0 + jnp.exp(-raw))) * norm
    )
    stacked = jnp.concatenate([grad_scale, grad_shape, jnp.zeros((6, here), F32)], axis=0)
    sm_send[0, 1:3, :] = jnp.dot(stacked, wide, precision=lax.Precision.HIGHEST, preferred_element_type=F32)[0:2]
    upright = stacked.T
    bias_sum = jnp.zeros((1, width), F32)
    for at in range(0, here, rows):
        gh = upright[at:at + rows, 0:1] * head_ref[0:1, :] + upright[at:at + rows, 1:2] * head_ref[1:2, :]
        gp = gh * slope[at:at + rows, :]
        bias_sum = bias_sum + jnp.sum(gp, axis=0, keepdims=True)
        pre[at:at + rows, :] = gp
    sm_send[0, 0:1, :] = bias_sum
    sm_send[0, 3:8, :] = jnp.zeros((5, width), F32)
    gp_bf = pre[...].astype(BF16)

    def grad_half(s):
        return lax.dot_general(agg[s], gp_bf, (((0,), (0,)), ((), ())), preferred_element_type=F32)

    if not pieces:
        gw_ref[0:half, :] = grad_half(0)
        gw_ref[half:, :] = grad_half(1)
        small_ref[...] = sm_send[0]
    else:
        big, mid, low = pieces

        def remote(src, dst, sems, at, peer):
            return pltpu.make_async_remote_copy(
                src_ref=src, dst_ref=dst, send_sem=sems[0].at[at], recv_sem=sems[1].at[at],
                device_id=peer, device_id_type=MESH,
            )

        gs, ss = (g_send, g_recv), (s_send, s_recv)
        partner = (mate, r)
        c_small = remote(sm_send.at[0], sm1, ss, 0, partner)
        start(c_small)
        g1s[...] = grad_half(1 - core).astype(BF16)
        c_big = remote(g1s, g1r, gs, 0, partner)
        start(c_big)
        mine = grad_half(core)
        c_small.wait_recv()
        sm_send[1] = sm_send[0] + sm1[...]
        small2 = [remote(sm_send.at[1], sm2.at[o - 1], ss, o, group_peer(o)) for o in range(1, group)]
        for copy in small2:
            start(copy)
        c_big.wait_recv()
        gsum[...] = mine + g1r[...].astype(F32)
        copies = []
        for o in range(1, group):
            other = lax.rem(in_group + o, group)
            g2s[o - 1] = gsum[pl.ds(pl.multiple_of(other * mid, mid), mid), :].astype(BF16)
            copy = remote(g2s.at[o - 1], g2r.at[o - 1], gs, o, group_peer(o))
            start(copy)
            copies.append(copy)
        for copy in small2:
            copy.wait_recv()
        total = sm_send[1]
        for o in range(1, group):
            total = total + sm2[o - 1]
        sm_send[2] = total
        small3 = [remote(sm_send.at[2], sm3.at[o - 1], ss, group - 1 + o, line_peer(o)) for o in range(1, line)]
        for copy in small3:
            start(copy)
        first_row = pl.multiple_of(in_group * mid, mid)
        for copy in copies:
            copy.wait_recv()
        total = gsum[pl.ds(first_row, mid), :]
        for o in range(1, group):
            total = total + g2r[o - 1].astype(F32)
        gsum[pl.ds(first_row, mid), :] = total
        copies = []
        for o in range(1, line):
            other = lax.rem(z + o, line)
            g3s[o - 1] = gsum[pl.ds(pl.multiple_of(first_row + other * low, low), low), :].astype(BF16)
            copy = remote(g3s.at[o - 1], g3r.at[o - 1], gs, group - 1 + o, line_peer(o))
            start(copy)
            copies.append(copy)
        for copy in small3:
            copy.wait_recv()
        total = sm_send[2]
        for o in range(1, line):
            total = total + sm3[o - 1]
        small_ref[...] = total
        for copy in copies:
            copy.wait_recv()
        total = gsum[pl.ds(pl.multiple_of(first_row + z * low, low), low), :]
        for o in range(1, line):
            total = total + g3r[o - 1].astype(F32)
        base = core * big
        spot = pl.multiple_of(base + first_row + z * low, low)
        gw_ref[pl.ds(spot, low), :] = total.astype(BF16)
        used = group + line - 1
        for o in range(1, line):
            ref = gw_ref.at[pl.ds(spot, low)]
            start(remote(ref, ref, gs, used + o - 1, line_peer(o)))
        for o in range(1, line):
            other = lax.rem(z + line - o, line)
            ref = gw_ref.at[pl.ds(pl.multiple_of(base + first_row + other * low, low), low)]
            remote(ref, ref, gs, used + o - 1, line_peer(o)).wait_recv()
        used = used + line - 1
        for o in range(1, group):
            ref = gw_ref.at[pl.ds(pl.multiple_of(base + first_row, mid), mid)]
            start(remote(ref, ref, gs, used + o - 1, group_peer(o)))
        for o in range(1, group):
            other = lax.rem(in_group + group - o, group)
            ref = gw_ref.at[pl.ds(pl.multiple_of(base + other * mid, mid), mid)]
            remote(ref, ref, gs, used + o - 1, group_peer(o)).wait_recv()
        used = used + group - 1
        ref = gw_ref.at[pl.ds(pl.multiple_of(base, big), big)]
        start(remote(ref, ref, gs, used, partner))
        ref = gw_ref.at[pl.ds(pl.multiple_of((1 - core) * big, big), big)]
        remote(ref, ref, gs, used, partner).wait_recv()
    for copy in sent:
        copy.wait_send()


def local(owners, replicas, features, tile_values, tile_rows, tile_cols, tile_counts, weight, bias, head, times, events):
    here, width = features.shape
    half = width // 2
    slots, tile = tile_values.shape[2], tile_values.shape[3]
    pieces = fused_sum_rows(owners, replicas, width)
    far = owners // 4
    group, line = 2 * replicas, max(owners // 4, 2)
    big, mid, low = pieces or (16, 16, 16)
    vmem = pl.BlockSpec(memory_space=pltpu.VMEM)
    smem = pl.BlockSpec(memory_space=pltpu.SMEM)
    hbm = pl.BlockSpec(memory_space=pl.ANY)
    dma = pltpu.SemaphoreType.DMA
    g_count = 2 * (group + line)
    hidden, grad_weight, small = pl.pallas_call(
        functools.partial(kernel, owners, replicas, pieces),
        out_shape=(
            jax.ShapeDtypeStruct((here, width), BF16),
            jax.ShapeDtypeStruct((width, width), BF16 if pieces else F32),
            jax.ShapeDtypeStruct((8, width), F32),
        ),
        in_specs=[hbm, hbm, smem, smem, smem, hbm, vmem, vmem, vmem, vmem],
        out_specs=(vmem, vmem, vmem),
        scratch_shapes=[
            pltpu.VMEM((2, owners, here, half), BF16),
            pltpu.VMEM((owners, here * replicas, here), BF16),
            pltpu.VMEM((slots + 1, tile, tile), BF16),
            pltpu.VMEM((width, width), BF16),
            pltpu.VMEM((2, replicas, here, half), F32),
            pltpu.VMEM((2, replicas - 1, here, half), BF16),
            pltpu.VMEM((2, replicas - 1, here, half), BF16),
            pltpu.VMEM((2, here, half), BF16),
            pltpu.VMEM((here, width), F32),
            pltpu.VMEM((here, width), F32),
            pltpu.VMEM((big, width), F32),
            pltpu.VMEM((big, width), BF16),
            pltpu.VMEM((big, width), BF16),
            pltpu.VMEM((group - 1, mid, width), BF16),
            pltpu.VMEM((group - 1, mid, width), BF16),
            pltpu.VMEM((line - 1, low, width), BF16),
            pltpu.VMEM((line - 1, low, width), BF16),
            pltpu.VMEM((3, 8, width), F32),
            pltpu.VMEM((8, width), F32),
            pltpu.VMEM((group - 1, 8, width), F32),
            pltpu.VMEM((line - 1, 8, width), F32),
            dma((4,)),
            dma((2, 2, 2, far)),
            dma((2, 2, 2, far)),
            dma((2, 2, 2, far + 1)),
            dma((2, 2, 2, far + 1)),
            dma((2, replicas - 1)),
            dma((2, replicas - 1)),
            dma((g_count,)),
            dma((g_count,)),
            dma((group + line,)),
            dma((group + line,)),
        ],
        compiler_params=pltpu.CompilerParams(
            collective_id=0, has_side_effects=True, vmem_limit_bytes=60 * 1024 * 1024
        ),
    )(
        features,
        tile_values.reshape(slots, tile, tile),
        tile_rows,
        tile_cols,
        tile_counts,
        weight,
        bias.reshape(1, width),
        head,
        times.reshape(1, here),
        events.reshape(1, here),
    )
    if pieces:
        grad_weight = grad_weight.astype(F32)
    else:
        grad_weight, small = lax.psum((grad_weight, small), ("blk", "rep"))
    return hidden, grad_weight, small[0], small[1:3]


def solution(mesh):
    placed = (
        P(("blk", "rep"), None),
        P("blk", "rep", None, None, None),
        P("blk", "rep", None),
        P("blk", "rep", None),
        P("blk", "rep"),
        P(),
        P(),
        P(),
        P(("blk", "rep")),
        P(("blk", "rep")),
    )
    return jax.shard_map(
        functools.partial(local, mesh.shape["blk"], mesh.shape["rep"]),
        mesh=mesh,
        in_specs=placed,
        out_specs=(P(("blk", "rep"), None), P(), P(), P()),
        check_vma=False,
    )
```

time: 368 us -> 78.2 us (0.21)
  waiting for transfers between devices: 180 us -> 0 us
  Pallas kernels: 0 us -> 70.1 us
  other arithmetic: 69.1 us -> 2.14 us
  blocking collectives: 39.3 us -> 0 us
  matrix products: 36.8 us -> 0 us
  between operations: 15.6 us -> 1.29 us
  loops' own time: 10.9 us -> 0 us
  starting transfers between devices: 9.43 us -> 0 us
    psum x1 -> x0, waiting for transfers between devices: 92.5 us -> none  [local(): totals = lax.psum((grad_weight, grad_bias, grad_head), ('blk', 'rep'))]
    pallas_call x0 -> x1, Pallas kernels: none -> 70.1 us  [local(): pl.pallas_call(functools.partial(kernel, owners, replicas, pieces), out_s...]
    ppermute x15 -> x0, waiting for transfers between devices: 62.2 us -> none  [passed_along(): return lax.ppermute(value, axis, pairs)]
    psum x1 -> x0, blocking collectives: 39.3 us -> none  [local(): totals = lax.psum((grad_weight, grad_bias, grad_head), ('blk', 'rep'))]
    dot_general x36 -> x0, matrix products: 36.8 us -> none  [the longest x16 25.5 us: add_capacity(): jnp.einsum('kij,kjf->kif', taken, chosen, preferred_element_type=jnp.floa...]
    reduce_scatter x1 -> x0, waiting for transfers between devices: 24.8 us -> none  [local(): lax.psum_scatter(partial_value.reshape(row_tiles * tile_size, feature_wid...]
    scatter-add x16 -> x0, other arithmetic: 24.7 us -> none  [add_capacity(): return partial_value.at[picked_rows].add(products)]
    reduce_sum x17 -> x0, other arithmetic: 20.9 us -> none  [the longest x16 20.6 us: run_bounds(): run_stop = jnp.sum(in_use & (col_ids < (source + 1) * col_tiles))]
  transfers between devices with their start and end apart: 17 -> 0, of which waited for: 15 -> 0; matrix products, arithmetic and copies ran while one was open for 11% -> 0% of each run, Pallas kernels for 0% -> 0%
where the time goes in v1:
time: 78.2 us; the launch traced here: 77.8 us
  Pallas kernels  70.1 us (90%)
  local copies, waits for them, and re-layouts  4.28 us (5%)
  other arithmetic  2.14 us (3%)
  between operations  1.29 us (2%)
    pallas_call x1, Pallas kernels, local(): pl.pallas_call(functools.partial(kernel, owners, replicas, pieces), out_s...  70.1 us
    slice x2, local copies, waits for them, and re-layouts, local(): return (hidden, grad_weight, small[0], small[1:3])  2.61 us
    convert_element_type x1, other arithmetic, local(): grad_weight = grad_weight.astype(F32)  2.14 us
    unnamed x1, local copies, waits for them, and re-layouts  1.67 us

profile of v1, /device:TPU:1, one launch (start us, length us, event | category | flops | bytes accessed | tf_op | source)
XLA Modules:
  0.0 77.8 jit_solution(10276403310096514866)
XLA Ops:
  1.3 70.1 %shard_map.129 = (bf16[256,512]{1,0:T(8,128)(2,1)}, bf16[512,512]{1,0:T(8,128)(2,1)}, f32[8,512]{1,0:T(8,128)}) custom-call(bf16[256,512]{1,0:T(8,128)(2,1)} %feats.1, bf16[96,128,128]{2,1,0:T(8,128)(2,1)} %bitcast.5, s32[1,1,96]{2,1,0:T(1,128)} %rows_ref.1, s32[1,1,96]{2,1,0:T(1,128)} %cols_ref.1, s32[1,1]{1,0:T(1,128)S(6)} %copy.15.count_ref, ...), custom_call_target="tpu_custom_call" | custom-call | tf_op jit(solution)/shard_map/pallas_call | solution.py:391
  71.4 1.3 %slice.6 = f32[1,512]{1,0:T(1,128)} slice(f32[8,512]{1,0:T(8,128)} %get-tuple-element.9), slice={[0:1], [0:512]} | slice | bytes 4096 | tf_op jit(solution)/shard_map/slice | solution.py:453
  72.7 1.3 %slice.7 = f32[2,512]{1,0:T(2,128)} slice(f32[8,512]{1,0:T(8,128)} %get-tuple-element.9), slice={[1:3], [0:512]} | slice | bytes 8192 | tf_op jit(solution)/shard_map/slice | solution.py:453
  74.0 2.1 %convert_element_type.3 = f32[512,512]{1,0:T(8,128)} convert(bf16[512,512]{1,0:T(8,128)(2,1)} %get-tuple-element.8) | non-fusion elementwise | flops 262144 | bytes 1572864 | tf_op jit(solution)/shard_map/convert_element_type | solution.py:450
  76.1 1.7 %copy.16 = bf16[256,512]{1,0:T(8,128)(2,1)} copy(bf16[256,512]{1,0:T(8,128)(2,1)} %get-tuple-element.14) | data formatting | bytes 524288

commit v2 on v1

--- a/solution.py
+++ b/solution.py
@@ -27,7 +27,7 @@
     owners, replicas, pieces,
     feats, tiles_hbm, rows_ref, cols_ref, count_ref, weight_hbm, bias_ref, head_ref, times_ref, events_ref,
     hidden_ref, gw_ref, small_ref,
-    gath, dense, tiles, weight, acc, xsend, xrecv, agg, pre, slope,
+    gath, dense, tiles, weight, acc, xsend0, xrecv0, xsend1, xrecv1, agg, pre, slope,
     gsum, g1s, g1r, g2s, g2r, g3s, g3r, sm_send, sm1, sm2, sm3,
     local_sem, ring_send, ring_recv, mate_send, mate_recv, x_send, x_recv, g_send, g_recv, s_send, s_recv,
 ):
@@ -181,7 +181,7 @@
 
     def to_rep(s, o):
         return pltpu.make_async_remote_copy(
-            src_ref=xsend.at[s, o - 1], dst_ref=xrecv.at[s, o - 1],
+            src_ref=(xsend0, xsend1)[s].at[o - 1], dst_ref=(xrecv0, xrecv1)[s].at[o - 1],
             send_sem=x_send.at[s, o - 1], recv_sem=x_recv.at[s, o - 1],
             device_id=(b, lax.rem(r + o, replicas)), device_id_type=MESH,
         )
@@ -190,7 +190,7 @@
         total = acc[s, r]
         for o in range(1, replicas):
             to_rep(s, o).wait_recv()
-            total = total + xrecv[s, o - 1].astype(F32)
+            total = total + (xrecv0, xrecv1)[s][o - 1].astype(F32)
         agg[s] = total.astype(BF16)
 
     own[0].wait()
@@ -199,14 +199,16 @@
     get_tiles.wait()
     first = jnp.int32(0)
     share = owners // far
+    acc[1] = jnp.zeros((replicas, here, half), F32)
     for h in range(1, far + 1):
         first = lax.fori_loop((h - 1) * share, h * share, fill, first)
         arrive(0, h)
-        if h == far - 1:
+        if h == 1:
             send_own(1)
+        else:
+            arrive(1, h - 1)
     for h in range(far + 1):
         arrive_mate(0, h)
-    arrive(1, 1)
 
     def first_half(part):
         def step(block, total):
@@ -214,31 +216,24 @@
         return lax.fori_loop(0, owners, step, jnp.zeros((here, half), F32))
 
     for o in range(1, replicas):
-        xsend[0, o - 1] = first_half(lax.rem(r + o, replicas)).astype(BF16)
+        xsend0[o - 1] = first_half(lax.rem(r + o, replicas))
         start(to_rep(0, o))
-    acc[0, r] = first_half(r)
-
-    arrive(1, 2)
-    acc[1] = jnp.zeros((replicas, here, half), F32)
-    for h in range(2):
+    arrive(1, far)
+    for h in range(far):
         arrive_mate(1, h)
         for part in range(replicas):
             multiply(1, part, blocks_at(h))
-    settle(0)
-    get_weight.wait()
-    pre[...] = jnp.dot(agg[0], weight[0:half, :], preferred_element_type=F32) + bias_ref[...]
-    for h in range(3, far + 1):
-        arrive(1, h)
-        arrive_mate(1, h - 1)
-        for part in range(replicas):
-            multiply(1, part, blocks_at(h - 1))
     arrive_mate(1, far)
     for o in range(1, replicas):
         part = lax.rem(r + o, replicas)
         multiply(1, part, blocks_at(far))
-        xsend[1, o - 1] = acc[1, part].astype(BF16)
+        xsend1[o - 1] = acc[1, part].astype(BF16)
         start(to_rep(1, o))
+    acc[0, r] = first_half(r)
     multiply(1, r, blocks_at(far))
+    settle(0)
+    get_weight.wait()
+    pre[...] = jnp.dot(agg[0], weight[0:half, :], preferred_element_type=F32) + bias_ref[...]
     settle(1)
 
     rows = 64
@@ -293,86 +288,112 @@
 
         gs, ss = (g_send, g_recv), (s_send, s_recv)
         partner = (mate, r)
+        base = core * big
+
+        def from_group(o):
+            return lax.rem(in_group + group - o, group)
+
+        def from_line(o):
+            return lax.rem(z + line - o, line)
+
+        def piece(start_row, member, count):
+            return pl.ds(pl.multiple_of(start_row + member * count, count), count)
+
         c_small = remote(sm_send.at[0], sm1, ss, 0, partner)
         start(c_small)
         g1s[...] = grad_half(1 - core).astype(BF16)
-        c_big = remote(g1s, g1r, gs, 0, partner)
-        start(c_big)
-        mine = grad_half(core)
+        order = [lax.rem(in_group + o, group) for o in range(1, group)] + [in_group]
+        copies1 = []
+        for at, member in enumerate(order):
+            rows_of = piece(0, member, mid)
+            copies1.append(remote(g1s.at[rows_of], g1r.at[rows_of], gs, at, partner))
+            start(copies1[-1])
+        gsum[...] = grad_half(core)
         c_small.wait_recv()
         sm_send[1] = sm_send[0] + sm1[...]
         small2 = [remote(sm_send.at[1], sm2.at[o - 1], ss, o, group_peer(o)) for o in range(1, group)]
         for copy in small2:
             start(copy)
-        c_big.wait_recv()
-        gsum[...] = mine + g1r[...].astype(F32)
+        used = group
         copies = []
         for o in range(1, group):
-            other = lax.rem(in_group + o, group)
-            g2s[o - 1] = gsum[pl.ds(pl.multiple_of(other * mid, mid), mid), :].astype(BF16)
-            copy = remote(g2s.at[o - 1], g2r.at[o - 1], gs, o, group_peer(o))
-            start(copy)
-            copies.append(copy)
+            rows_of = piece(0, order[o - 1], mid)
+            copies1[o - 1].wait_recv()
+            g2s[o - 1] = (gsum[rows_of, :] + g1r[rows_of, :].astype(F32)).astype(BF16)
+            copies.append(remote(g2s.at[o - 1], g2r.at[o - 1], gs, used + o - 1, group_peer(o)))
+            start(copies[-1])
+        used += group - 1
+        copies1[group - 1].wait_recv()
+        first_row = in_group * mid
+        rows_of = piece(0, in_group, mid)
+        total = gsum[rows_of, :] + g1r[rows_of, :].astype(F32)
         for copy in small2:
             copy.wait_recv()
-        total = sm_send[1]
+        small_total = sm_send[1]
         for o in range(1, group):
-            total = total + sm2[o - 1]
-        sm_send[2] = total
+            small_total = small_total + sm2[o - 1]
+        sm_send[2] = small_total
         small3 = [remote(sm_send.at[2], sm3.at[o - 1], ss, group - 1 + o, line_peer(o)) for o in range(1, line)]
         for copy in small3:
             start(copy)
-        first_row = pl.multiple_of(in_group * mid, mid)
-        for copy in copies:
-            copy.wait_recv()
-        total = gsum[pl.ds(first_row, mid), :]
         for o in range(1, group):
+            copies[o - 1].wait_recv()
             total = total + g2r[o - 1].astype(F32)
-        gsum[pl.ds(first_row, mid), :] = total
+        gsum[rows_of, :] = total
         copies = []
         for o in range(1, line):
-            other = lax.rem(z + o, line)
-            g3s[o - 1] = gsum[pl.ds(pl.multiple_of(first_row + other * low, low), low), :].astype(BF16)
-            copy = remote(g3s.at[o - 1], g3r.at[o - 1], gs, group - 1 + o, line_peer(o))
-            start(copy)
-            copies.append(copy)
+            g3s[o - 1] = gsum[piece(first_row, lax.rem(z + o, line), low), :].astype(BF16)
+            copies.append(remote(g3s.at[o - 1], g3r.at[o - 1], gs, used + o - 1, line_peer(o)))
+            start(copies[-1])
+        used += line - 1
+        total = gsum[piece(first_row, z, low), :]
+        for o in range(1, line):
+            copies[o - 1].wait_recv()
+            total = total + g3r[o - 1].astype(F32)
+        gw_ref[piece(base + first_row, z, low), :] = total.astype(BF16)
+
+        def along_line(o, member):
+            ref = gw_ref.at[piece(base + first_row, member, low)]
+            return remote(ref, ref, gs, used + o - 1, line_peer(o))
+
+        def in_plane(o, lo, from_member):
+            ref = gw_ref.at[piece(base + from_member * mid, from_line(lo), low)]
+            return remote(ref, ref, gs, used + (line - 1) + (o - 1) * line + lo, group_peer(o))
+
+        def over_chip(o, lo, half_base):
+            ref = gw_ref.at[piece(half_base + from_group(o) * mid, from_line(lo), low)]
+            return remote(ref, ref, gs, used + (line - 1) + (group - 1) * line + o * line + lo, partner)
+
+        for o in range(1, line):
+            start(along_line(o, z))
+        for lo in range(line):
+            if lo:
+                along_line(lo, from_line(lo)).wait_recv()
+            for o in range(1, group):
+                start(in_plane(o, lo, in_group))
+            start(over_chip(0, lo, base))
         for copy in small3:
             copy.wait_recv()
-        total = sm_send[2]
+        small_total = sm_send[2]
         for o in range(1, line):
-            total = total + sm3[o - 1]
-        small_ref[...] = total
-        for copy in copies:
-            copy.wait_recv()
-        total = gsum[pl.ds(pl.multiple_of(first_row + z * low, low), low), :]
-        for o in range(1, line):
-            total = total + g3r[o - 1].astype(F32)
-        base = core * big
-        spot = pl.multiple_of(base + first_row + z * low, low)
-        gw_ref[pl.ds(spot, low), :] = total.astype(BF16)
-        used = group + line - 1
-        for o in range(1, line):
-            ref = gw_ref.at[pl.ds(spot, low)]
-            start(remote(ref, ref, gs, used + o - 1, line_peer(o)))
-        for o in range(1, line):
-            other = lax.rem(z + line - o, line)
-            ref = gw_ref.at[pl.ds(pl.multiple_of(base + first_row + other * low, low), low)]
-            remote(ref, ref, gs, used + o - 1, line_peer(o)).wait_recv()
-        used = used + line - 1
-        for o in range(1, group):
-            ref = gw_ref.at[pl.ds(pl.multiple_of(base + first_row, mid), mid)]
-            start(remote(ref, ref, gs, used + o - 1, group_peer(o)))
-        for o in range(1, group):
-            other = lax.rem(in_group + group - o, group)
-            ref = gw_ref.at[pl.ds(pl.multiple_of(base + other * mid, mid), mid)]
-            remote(ref, ref, gs, used + o - 1, group_peer(o)).wait_recv()
-        used = used + group - 1
-        ref = gw_ref.at[pl.ds(pl.multiple_of(base, big), big)]
-        start(remote(ref, ref, gs, used, partner))
-        ref = gw_ref.at[pl.ds(pl.multiple_of((1 - core) * big, big), big)]
-        remote(ref, ref, gs, used, partner).wait_recv()
+            small_total = small_total + sm3[o - 1]
+        small_ref[...] = small_total
+        for lo in range(line):
+            for o in range(1, group):
+                in_plane(o, lo, from_group(o)).wait_recv()
+                start(over_chip(o, lo, base))
+        for lo in range(line):
+            for o in range(group):
+                over_chip(o, lo, (1 - core) * big).wait_recv()
     for copy in sent:
         copy.wait_send()
+
+
+def finish(hidden_in, gw_in, small_in, hidden_out, gw_out, bias_out, head_out):
+    hidden_out[...] = hidden_in[...]
+    gw_out[...] = gw_in[...].astype(F32)
+    bias_out[...] = small_in[0, :]
+    head_out[...] = small_in[1:3, :]
 
 
 def local(owners, replicas, features, tile_values, tile_rows, tile_cols, tile_counts, weight, bias, head, times, events):
@@ -387,7 +408,7 @@
     smem = pl.BlockSpec(memory_space=pltpu.SMEM)
     hbm = pl.BlockSpec(memory_space=pl.ANY)
     dma = pltpu.SemaphoreType.DMA
-    g_count = 2 * (group + line)
+    g_count = 2 * group + 2 * line + 2 * group * line
     hidden, grad_weight, small = pl.pallas_call(
         functools.partial(kernel, owners, replicas, pieces),
         out_shape=(
@@ -403,8 +424,10 @@
             pltpu.VMEM((slots + 1, tile, tile), BF16),
             pltpu.VMEM((width, width), BF16),
             pltpu.VMEM((2, replicas, here, half), F32),
-            pltpu.VMEM((2, replicas - 1, here, half), BF16),
-            pltpu.VMEM((2, replicas - 1, here, half), BF16),
+            pltpu.VMEM((replicas - 1, here, half), F32),
+            pltpu.VMEM((replicas - 1, here, half), F32),
+            pltpu.VMEM((replicas - 1, here, half), BF16),
+            pltpu.VMEM((replicas - 1, here, half), BF16),
             pltpu.VMEM((2, here, half), BF16),
             pltpu.VMEM((here, width), F32),
             pltpu.VMEM((here, width), F32),
@@ -446,11 +469,19 @@
         times.reshape(1, here),
         events.reshape(1, here),
     )
-    if pieces:
-        grad_weight = grad_weight.astype(F32)
-    else:
+    if not pieces:
         grad_weight, small = lax.psum((grad_weight, small), ("blk", "rep"))
-    return hidden, grad_weight, small[0], small[1:3]
+    return pl.pallas_call(
+        finish,
+        out_shape=(
+            jax.ShapeDtypeStruct((here, width), BF16),
+            jax.ShapeDtypeStruct((width, width), F32),
+            jax.ShapeDtypeStruct((width,), F32),
+            jax.ShapeDtypeStruct((2, width), F32),
+        ),
+        in_specs=[vmem, vmem, vmem],
+        out_specs=(vmem, vmem, vmem, vmem),
+    )(hidden, grad_weight, small)
 
 
 def solution(mesh):

time: 78.2 us -> 68.5 us (0.88)
  local copies, waits for them, and re-layouts: 4.28 us -> 0 us
  Pallas kernels: 70.1 us -> 67 us
  other arithmetic: 2.14 us -> 0 us
    pallas_call x1, Pallas kernels: 70.1 us -> 64.8 us  [local(): pl.pallas_call(functools.partial(kernel, owners, replicas, pieces), out_s...]
    slice x2 -> x0, local copies, waits for them, and re-layouts: 2.61 us -> none  [local(): return (hidden, grad_weight, small[0], small[1:3])]
    pallas_call x0 -> x1, Pallas kernels: none -> 2.25 us  [local(): pl.pallas_call(finish, out_shape=(jax.ShapeDtypeStruct((here, width), BF1...]
    convert_element_type x1 -> x0, other arithmetic: 2.14 us -> none  [local(): grad_weight = grad_weight.astype(F32)]
    unnamed x1 -> x0, local copies, waits for them, and re-layouts: 1.67 us -> none
where the time goes in v2:
time: 68.5 us; the launch traced here: 68.3 us
  Pallas kernels  67 us (98%)
  between operations  1.29 us (2%)
    pallas_call x1, Pallas kernels, local(): pl.pallas_call(functools.partial(kernel, owners, replicas, pieces), out_s...  64.8 us
    pallas_call x1, Pallas kernels, local(): pl.pallas_call(finish, out_shape=(jax.ShapeDtypeStruct((here, width), BF1...  2.25 us

profile of v2, /device:TPU:1, one launch (start us, length us, event | category | flops | bytes accessed | tf_op | source)
XLA Modules:
  0.0 68.3 jit_solution(6148632800885400835)
XLA Ops:
  1.3 64.8 %shard_map.129 = (bf16[256,512]{1,0:T(8,128)(2,1)}, bf16[512,512]{1,0:T(8,128)(2,1)}, f32[8,512]{1,0:T(8,128)}) custom-call(bf16[256,512]{1,0:T(8,128)(2,1)} %feats.1, bf16[96,128,128]{2,1,0:T(8,128)(2,1)} %bitcast.4, s32[1,1,96]{2,1,0:T(1,128)} %rows_ref.1, s32[1,1,96]{2,1,0:T(1,128)} %cols_ref.1, s32[1,1]{1,0:T(1,128)S(6)} %copy.14.count_ref, ...), custom_call_target="tpu_custom_call" | custom-call | tf_op jit(solution)/shard_map/pallas_call | solution.py:412
  66.0 2.3 %shard_map.130 = (bf16[256,512]{1,0:T(8,128)(2,1)}, f32[512,512]{1,0:T(8,128)}, f32[512]{0:T(512)}, f32[2,512]{1,0:T(2,128)}) custom-call(bf16[256,512]{1,0:T(8,128)(2,1)} %get-tuple-element.7.hidden_in, bf16[512,512]{1,0:T(8,128)(2,1)} %get-tuple-element.8.gw_in, f32[8,512]{1,0:T(8,128)} %get-tuple-element.9.small_in), custom_call_target="tpu_custom_call" | custom-call | tf_op jit(solution)/shard_map/pallas_call | solution.py:474

commit v3 on v2

--- a/solution.py
+++ b/solution.py
@@ -173,6 +173,18 @@
             total = total + product(s, part, block)
         acc[s, part] = total
 
+    many = replicas > 2
+
+    def multiply_all(s, h):
+        if many:
+            def step(part, carry):
+                multiply(s, part, blocks_at(h))
+                return carry
+            lax.fori_loop(0, replicas, step, 0)
+        else:
+            for part in range(replicas):
+                multiply(s, part, blocks_at(h))
+
     def blocks_at(h):
         if h == 0:
             return [b, mate]
@@ -198,39 +210,45 @@
     send_own(0)
     get_tiles.wait()
     first = jnp.int32(0)
-    share = owners // far
-    acc[1] = jnp.zeros((replicas, here, half), F32)
+    acc[...] = jnp.zeros(acc.shape, F32)
+    first = lax.fori_loop(0, far, fill, first)
     for h in range(1, far + 1):
-        first = lax.fori_loop((h - 1) * share, h * share, fill, first)
         arrive(0, h)
         if h == 1:
             send_own(1)
-        else:
-            arrive(1, h - 1)
-    for h in range(far + 1):
-        arrive_mate(0, h)
-
-    def first_half(part):
-        def step(block, total):
-            return total + product(0, part, block)
-        return lax.fori_loop(0, owners, step, jnp.zeros((here, half), F32))
-
-    for o in range(1, replicas):
-        xsend0[o - 1] = first_half(lax.rem(r + o, replicas))
-        start(to_rep(0, o))
-    arrive(1, far)
-    for h in range(far):
-        arrive_mate(1, h)
-        for part in range(replicas):
-            multiply(1, part, blocks_at(h))
-    arrive_mate(1, far)
+            lax.fori_loop(far, owners, fill, first)
+            continue
+        arrive(1, h - 1)
+        for done in range(h - 2, h) if h == 2 else (h - 1,):
+            arrive_mate(0, done)
+            multiply_all(0, done)
+        arrive_mate(1, h - 2)
+        multiply_all(1, h - 2)
+    arrive_mate(0, far)
+    if many:
+        multiply_all(0, far)
     for o in range(1, replicas):
         part = lax.rem(r + o, replicas)
-        multiply(1, part, blocks_at(far))
+        if not many:
+            multiply(0, part, blocks_at(far))
+        xsend0[o - 1] = acc[0, part]
+        start(to_rep(0, o))
+    arrive_mate(1, far - 1)
+    multiply_all(1, far - 1)
+    arrive(1, far)
+    if not many:
+        multiply(0, r, blocks_at(far))
+    arrive_mate(1, far)
+    if many:
+        multiply_all(1, far)
+    for o in range(1, replicas):
+        part = lax.rem(r + o, replicas)
+        if not many:
+            multiply(1, part, blocks_at(far))
         xsend1[o - 1] = acc[1, part].astype(BF16)
         start(to_rep(1, o))
-    acc[0, r] = first_half(r)
-    multiply(1, r, blocks_at(far))
+    if not many:
+        multiply(1, r, blocks_at(far))
     settle(0)
     get_weight.wait()
     pre[...] = jnp.dot(agg[0], weight[0:half, :], preferred_element_type=F32) + bias_ref[...]

time: 68.5 us -> 65.7 us (0.959)
  Pallas kernels: 67 us -> 64.3 us
    pallas_call x1, Pallas kernels: 64.8 us -> 62 us  [local(): pl.pallas_call(functools.partial(kernel, owners, replicas, pieces), out_s...]
where the time goes in v3:
time: 65.7 us; the launch traced here: 65.6 us
  Pallas kernels  64.3 us (98%)
  between operations  1.29 us (2%)
    pallas_call x1, Pallas kernels, local(): pl.pallas_call(functools.partial(kernel, owners, replicas, pieces), out_s...  62 us
    pallas_call x1, Pallas kernels, local(): pl.pallas_call(finish, out_shape=(jax.ShapeDtypeStruct((here, width), BF1...  2.25 us

profile of v3, /device:TPU:1, one launch (start us, length us, event | category | flops | bytes accessed | tf_op | source)
XLA Modules:
  0.0 65.6 jit_solution(7568637558517789117)
XLA Ops:
  1.3 62.0 %shard_map.129 = (bf16[256,512]{1,0:T(8,128)(2,1)}, bf16[512,512]{1,0:T(8,128)(2,1)}, f32[8,512]{1,0:T(8,128)}) custom-call(bf16[256,512]{1,0:T(8,128)(2,1)} %feats.1, bf16[96,128,128]{2,1,0:T(8,128)(2,1)} %bitcast.4, s32[1,1,96]{2,1,0:T(1,128)} %rows_ref.1, s32[1,1,96]{2,1,0:T(1,128)} %cols_ref.1, s32[1,1]{1,0:T(1,128)S(6)} %copy.14.count_ref, ...), custom_call_target="tpu_custom_call" | custom-call | tf_op jit(solution)/shard_map/pallas_call | solution.py:430
  63.3 2.3 %shard_map.130 = (bf16[256,512]{1,0:T(8,128)(2,1)}, f32[512,512]{1,0:T(8,128)}, f32[512]{0:T(512)}, f32[2,512]{1,0:T(2,128)}) custom-call(bf16[256,512]{1,0:T(8,128)(2,1)} %get-tuple-element.7.hidden_in, bf16[512,512]{1,0:T(8,128)(2,1)} %get-tuple-element.8.gw_in, f32[8,512]{1,0:T(8,128)} %get-tuple-element.9.small_in), custom_call_target="tpu_custom_call" | custom-call | tf_op jit(solution)/shard_map/pallas_call | solution.py:492
